TPU v7x, 256 devices: a whole 4x4x8 slice. The times are simulated.
256 devices in a mesh: seq: 32 (over z, x), clip: 8 (over y, core).
Axes of the slice: x: 4, y: 4, z: 8, core: 2. Of those that a mesh axis runs over, the one named last changes fastest.
Arguments:
- tokens: bfloat16 [8, 16384, 1280], P('clip', 'seq'), may hold values from -24 to 24
- slot_weight: bfloat16 [1280, 256], replicated, may hold values from -2 to 2
- pattern: int32 [128, 16], P('seq'), may hold values from 0 to 63, all different within a row
- w_in: bfloat16 [64, 1280, 5120], P('seq', None, 'clip'), may hold values from -0.15625 to 0.15625
- w_out: bfloat16 [64, 5120, 1280], P('seq', 'clip'), may hold values from -0.078125 to 0.078125
Outputs:
- mixed: bfloat16 [8, 16384, 1280], P('clip', 'seq')
Inputs may be any that keep to these rules, and one draw needn't show every extreme that they name: `pattern`: each row names 16 different groups, and every group is named by some row.
All inputs are finite; a program needn't handle non-finite values.
Results may differ from a plain program's by a relative error of at most 0.0095.
Values may be sent and summed in bfloat16 or wider, within the bound.
A program may use at most 128 MiB of HBM per device.

v0:
```python
import jax
import jax.numpy as jnp
from jax import lax
from jax.sharding import PartitionSpec as P

SLOTS = 4
BLOCK = 128


very_low = -1e30


def entering(value, axis, join, neutral):
    count, mine = (lax.axis_size(axis), lax.axis_index(axis))
    pieces = jax.tree.map(lambda part: lax.all_gather(part, axis), value)
    running = jax.tree.map(
        lambda part, zero: jnp.full_like(part, 0) + jnp.asarray(zero, part.dtype), value, neutral
    )

    def turn(position, running):
        longer = join(running, jax.tree.map(lambda part: part[position], pieces))
        return jax.tree.map(lambda new, old: jnp.where(position < mine, new, old), longer, running)

    return lax.fori_loop(0, count - 1, turn, running)


def spread(array, axis, root):
    mine = lax.axis_index(axis) == root
    return lax.psum(jnp.where(mine, array, jnp.zeros_like(array)), axis)


def join_states(earlier, later):
    top = jnp.maximum(earlier[0], later[0])
    scale_early = jnp.exp(earlier[0] - top)
    scale_late = jnp.exp(later[0] - top)
    mass = earlier[1] * scale_early + later[1] * scale_late
    weighted = earlier[2] * scale_early[:, :, None] + later[2] * scale_late[:, :, None]
    return (top, mass, weighted)


def local(tokens, slot_weight, pattern, w_in, w_out):
    clip_rows, tok_rows, width = tokens.shape
    total_slots = slot_weight.shape[1]
    seq_count = lax.axis_size("seq")
    own_slots = total_slots // seq_count
    blocks = tok_rows // BLOCK
    logits = jnp.einsum("ctd,ds->cts", tokens, slot_weight, preferred_element_type=jnp.float32)
    groups = jnp.arange(total_slots, dtype=jnp.int32) // SLOTS
    allowed = jnp.any(pattern[:, :, None] == groups[None, None, :], axis=1)
    tiled = logits.reshape(clip_rows, blocks, BLOCK, total_slots)
    block_top = jnp.max(tiled, axis=2)
    weights = jnp.exp(tiled - block_top[:, :, None, :]) * allowed[None, :, None, :].astype(
        jnp.float32
    )
    masses = jnp.sum(weights, axis=2)
    peak = jnp.where(allowed[None], block_top, very_low)
    partial_value = jnp.einsum(
        "cbts,cbtd->cbsd",
        weights.astype(jnp.bfloat16),
        tokens.reshape(clip_rows, blocks, BLOCK, width),
        preferred_element_type=jnp.float32,
    )
    first_slot = lax.axis_index("seq") * own_slots
    local_top = jnp.max(peak, axis=1)
    factor = jnp.exp(peak - local_top[:, None, :])
    weighted = jnp.einsum("cbs,cbsd->csd", factor, partial_value, precision=lax.Precision.HIGHEST)
    mass = jnp.sum(factor * masses, axis=1)
    state = (local_top, mass, weighted)
    empty = (jnp.full_like(local_top, very_low), jnp.zeros_like(mass), jnp.zeros_like(weighted))
    before = entering(state, "seq", join_states, empty)
    joined = join_states(before, state)
    safe_mass = jnp.where(joined[1] > 0.0, joined[1], 1.0)
    ready = (joined[2] / safe_mass[:, :, None]).astype(jnp.bfloat16)
    whole = spread(ready, "seq", seq_count - 1)
    mine = lax.dynamic_slice_in_dim(whole, first_slot, own_slots, 1)
    piece = lax.all_gather(mine, "clip", axis=0, tiled=True)
    count = piece.shape[0]
    grouped = piece.reshape(count, w_in.shape[0], SLOTS, width)
    inner = jnp.einsum("necd,edf->necf", grouped, w_in, preferred_element_type=jnp.float32)
    active = jax.nn.gelu(inner, approximate=True).astype(jnp.bfloat16)
    outer = jnp.einsum("necf,efd->necd", active, w_out, preferred_element_type=jnp.float32)
    produced = outer.reshape(count, own_slots, width)
    slot_out = lax.psum_scatter(produced, "clip", scatter_dimension=0, tiled=True).astype(
        jnp.bfloat16
    )
    probs = jax.nn.softmax(logits, axis=-1).astype(jnp.bfloat16)
    mixed = jnp.einsum(
        "cts,csd->ctd",
        probs,
        lax.all_gather(slot_out, "seq", axis=1, tiled=True),
        preferred_element_type=jnp.float32,
    )
    return mixed.astype(jnp.bfloat16)


def solution(mesh):
    in_specs = (
        P("clip", "seq", None),
        P(),
        P("seq", None),
        P("seq", None, "clip"),
        P("seq", "clip", None),
    )
    out_specs = P("clip", "seq", None)
    return jax.shard_map(local, mesh=mesh, in_specs=in_specs, out_specs=out_specs, check_vma=False)
```

profile of v0, /device:TPU:2, one launch (start us, length us, event | category | flops | bytes accessed | tf_op | source)
XLA Modules:
  0.0 667.0 jit_solution(3661416673026067336)
XLA Ops:
  15.0 11.6 %fusion.4 = f32[256,1,1280]{2,1,0:T(1,128)S(1)} fusion(f32[4,256,1]{0,2,1:T(1,128)S(1)} %copy.19, f32[4,256,1280]{2,1,0:T(8,128)S(1)} %fusion.20), kind=kOutput, calls=%fused_computation.14 | convolution fusion | flops 15728640 | bytes 6557696 | tf_op jit(solution)/shard_map/cbs,cbsd->csd/dot_general | solution.py:66
  28.3 45.6 %all-gather.4 = f32[32,1,256]{2,1,0:T(1,128)S(1)} all-gather(f32[1,1,256]{2,1,0:T(1,128)S(1)} %bitcast.119), channel_id=3, replica_groups=mesh['seq'=32,'clip'=8] {'seq'}, dimensions={0}, use_global_device_ids=true | all-gather | bytes 33792 | tf_op jit(solution)/shard_map/all_gather | solution.py:15
  73.9 40.6 %all-gather.3 = f32[32,1,256]{2,1,0:T(1,128)S(1)} all-gather(f32[1,1,256]{2,1,0:T(1,128)S(1)} %bitcast.117), channel_id=2, replica_groups=mesh['seq'=32,'clip'=8] {'seq'}, dimensions={0}, use_global_device_ids=true | all-gather | bytes 33792 | tf_op jit(solution)/shard_map/all_gather | solution.py:15
  114.5 198.8 %all-gather.7.cloned.1.call-done = f32[8192,1280]{1,0:T(8,128)} async-done(((f32[256,1280]{1,0:T(8,128)}), f32[8192,1280]{1,0:T(8,128)}) %all-gather.7.cloned.1.call-update) | async-done | bytes 41943056 | tf_op jit(solution)/shard_map/all_gather | solution.py:15
  313.3 94.7 %while.18 = (s32[]{:T(128)}, f32[1,256]{1,0:T(1,128)S(1)}, f32[1,256]{1,0:T(1,128)S(1)}, f32[1,256,1280]{2,1,0:T(8,128)}, s32[]{:T(128)}, /*index=5*/f32[32,1,25...) while((s32[]{:T(128)}, f32[1,256]{1,0:T(1,128)S(1)}, ...), condition=%wide.region_8.9_spmd.clone, body=%wide.region_7.8_spmd.clone.sunk | while | flops 1640964 | bytes 3942531 | solution.py:24
  316.0 3.0 fusion.59
  319.0 3.0 fusion.59
  325.2 3.0 fusion.59
  328.2 3.0 fusion.59
  331.3 3.0 fusion.59
  334.4 3.0 fusion.59
  337.4 3.0 fusion.59
  340.5 3.0 fusion.59
  343.6 3.0 fusion.59
  346.6 3.0 fusion.59
  349.7 3.0 fusion.59
  352.8 3.0 fusion.59
  358.9 3.0 fusion.59
  362.0 3.0 fusion.59
  411.0 145.4 %all-reduce.2.cloned.1.call-done = bf16[1,256,1280]{2,1,0:T(8,128)(2,1)} async-done(((bf16[1,256,1280]{2,1,0:T(8,128)(2,1)}), bf16[1,256,1280]{2,1,0:T(8,128)(2,1)}) %all-reduce.2.cloned.1.call-update) | async-done | bytes 655376 | tf_op jit(solution)/shard_map/psum | solution.py:29
  557.1 13.1 %all_gather.30 = bf16[8,8,1280]{2,1,0:T(8,128)(2,1)S(1)} all-gather(bf16[1,8,1280]{2,1,0:T(8,128)(2,1)S(1)} %constant_dynamic-slice_fusion.1), channel_id=1, replica_groups=mesh['seq'=32,'clip'=8] {'clip'}, dimensions={0}, use_global_device_ids=true | all-gather | bytes 184320 | tf_op jit(solution)/shard_map/all_gather | solution.py:76
  570.2 3.8 fusion.6
  578.3 28.8 %reduce-scatter.2.cloned.1.call-done = f32[1,8,1280]{2,1,0:T(8,128)} async-done(((f32[8,8,1280]{2,1,0:T(8,128)}), f32[1,8,1280]{2,1,0:T(8,128)}) %reduce-scatter.2.cloned.1.call-update) | async-done | bytes 40976 | tf_op jit(solution)/shard_map/reduce_scatter | solution.py:83
  607.9 49.9 %all_gather.31 = bf16[1,256,1280]{2,1,0:T(8,128)(2,1)S(1)} all-gather(bf16[1,8,1280]{2,1,0:T(8,128)(2,1)S(1)} %convert_element_type.38), channel_id=1, replica_groups=mesh['seq'=32,'clip'=8] {'seq'}, dimensions={1}, use_global_device_ids=true | all-gather | bytes 675840 | tf_op jit(solution)/shard_map/all_gather | solution.py:90
  (83 shorter events, 73.6 us)
Async XLA Ops:
  6.5 563.7 %copy-start = (bf16[2,640,1280]{2,1,0:T(8,128)(2,1)S(1)}, bf16[2,640,1280]{2,1,0:T(8,128)(2,1)}, u32[]{:S(2)}) copy-start(bf16[2,640,1280]{2,1,0:T(8,128)(2,1)} %param.11) | copy-start | bytes 9830404
  6.5 306.7 %all-gather.7.cloned.1.call-start = ((), (), s32[]{:S(2)}) async-start(), calls=%async_computation.3 | async-start | bytes 43253760 | tf_op jit(solution)/shard_map/all_gather | solution.py:15
  9.5 0.8 copy-start.1
  26.7 1.5 copy-start.2
  28.2 528.2 %all-reduce.2.cloned.1.call-start = ((), (), s32[]{:S(2)}) async-start(), calls=%async_computation.1 | async-start | bytes 1310720 | tf_op jit(solution)/shard_map/psum | solution.py:29
  410.9 196.2 %reduce-scatter.2.cloned.1.call-start = ((), (), s32[]{:S(2)}) async-start(), calls=%async_computation.2 | async-start | bytes 368640 | tf_op jit(solution)/shard_map/reduce_scatter | solution.py:83
Sparse Core Ops, SparseCore 0:
  28.3 284.9 all-gather.6
  411.0 145.3 all-reduce.1
  575.9 31.0 reduce-scatter.1
where the time goes:
time: 669 us; the launch traced here: 667 us
  waiting for transfers between devices  373 us (56%)
  blocking collectives  149 us (22%)
  other arithmetic  102 us (15%)
  matrix products  22.5 us (3%)
  between operations  13.2 us (2%)
  local copies, waits for them, and re-layouts  6.97 us (1%)
    all_gather x1, waiting for transfers between devices, entering(): pieces = jax.tree.map(lambda part: lax.all_gather(part, axis), value)  199 us
    psum x1, waiting for transfers between devices, spread(): return lax.psum(jnp.where(mine, array, jnp.zeros_like(array)), axis)  145 us
    select_n x62, other arithmetic, turn(): jnp.where(position < mine, new, old)  94.7 us
    all_gather x2, blocking collectives, entering(): pieces = jax.tree.map(lambda part: lax.all_gather(part, axis), value)  86.2 us
    all_gather x1, blocking collectives, local(): lax.all_gather(slot_out, 'seq', axis=1, tiled=True)  49.9 us
    reduce_scatter x1, waiting for transfers between devices, local(): lax.psum_scatter(produced, 'clip', scatter_dimension=0, tiled=True)  28.8 us
  transfers between devices with their start and end apart: 3, of which 3 were waited for; matrix products, arithmetic and copies ran while one was open for 0% of the time, Pallas kernels for 0%

commit v1 on v0

v1 whole, which is shorter than its diff:
```python
import functools

import jax
import jax.numpy as jnp
from jax import lax
from jax.experimental import pallas as pl
from jax.experimental.pallas import tpu as pltpu
from jax.sharding import PartitionSpec as P

MESH = pl.DeviceIdType.MESH
BF16, F32 = jnp.bfloat16, jnp.float32
D = 1280
FS = 640
TOK = 512
SLOTS_ALL = 256
ZN, XN, YN = 8, 4, 4
CLIPS = 8
EXT = 128
CHUNKS = (512, 512, 256)
STARTS = tuple(sum(CHUNKS[:i]) for i in range(len(CHUNKS)))
NC = len(CHUNKS)
LOW = -1.0e30
EMPTY = -1.0e29

XP = (2, 1, 3)
ZP = (4, 3, 5, 2, 6, 1, 7)
CP = tuple(range(1, 8))


def pieces(v):
    hi = v.astype(BF16).astype(F32)
    mid = (v - hi).astype(BF16).astype(F32)
    lo = ((v - hi) - mid).astype(BF16).astype(F32)
    return hi, mid, lo


def ext_of(top, mass):
    lane = lax.broadcasted_iota(jnp.int32, (top.shape[0], EXT), 1)
    out = jnp.zeros((top.shape[0], EXT), F32)
    for i, piece in enumerate(pieces(top) + pieces(mass)):
        out = jnp.where(lane == i, piece, out)
    return out


def of_ext(ext):
    e = ext.astype(F32)
    return e[:, 0:1] + e[:, 1:2] + e[:, 2:3], e[:, 3:4] + e[:, 4:5] + e[:, 5:6]


def merge(stats):
    top = stats[0][0]
    for t, _ in stats[1:]:
        top = jnp.maximum(top, t)
    factors = [jnp.exp(t - top) for t, _ in stats]
    mass = factors[0] * stats[0][1]
    for f, (_, m) in zip(factors[1:], stats[1:]):
        mass = mass + f * m
    return factors, top, mass


def pack(v):
    h = v.shape[-1] // 2
    return jnp.concatenate([v[:, :, :h], v[:, :, h:]], axis=1)


def unpack(v):
    n, _, h = v.shape
    f = v.astype(F32)
    return jnp.concatenate([f[:, :8].reshape(n * 8, h), f[:, 8:].reshape(n * 8, h)], axis=1)


def kernel(tok_hbm, sw_hbm, pat_ref, win_hbm, wout_hbm, out_hbm, *scratch):
    it = iter(scratch)
    tok, sw, win, wout = next(it), next(it), next(it), next(it)
    wt_ref, probs, outv = next(it), next(it), next(it)
    psend = [next(it) for _ in range(NC)]
    xbuf = [next(it) for _ in range(NC)]
    zsend = [next(it) for _ in range(NC)]
    zbuf = [next(it) for _ in range(NC)]
    ybuf = [next(it) for _ in range(NC)]
    rsend = [next(it) for _ in range(NC)]
    rbuf = [next(it) for _ in range(NC)]
    agx = [next(it) for _ in range(NC)]
    load_sem, out_sem, send_sem, recv_sem = next(it), next(it), next(it), next(it)

    seq, clip = lax.axis_index("seq"), lax.axis_index("clip")
    z, x = seq // XN, seq % XN
    y, core = clip // 2, clip % 2

    def x_peer(d):
        return {"seq": z * XN + (x + d) % XN, "clip": clip}

    def z_peer(d):
        return {"seq": ((z + d) % ZN) * XN + x, "clip": clip}

    def c_peer(j):
        return {"seq": seq, "clip": ((y + j // 2) % YN) * 2 + (core + j % 2) % 2}

    def c_back(j):
        return {"seq": seq, "clip": ((y + YN - j // 2) % YN) * 2 + (core + j % 2) % 2}

    loads = [
        pltpu.make_async_copy(sw_hbm, sw, load_sem.at[0]),
        pltpu.make_async_copy(tok_hbm, tok, load_sem.at[1]),
        pltpu.make_async_copy(win_hbm, win, load_sem.at[2]),
        pltpu.make_async_copy(wout_hbm, wout, load_sem.at[3]),
    ]
    for load in loads:
        load.start()

    barrier = pltpu.get_barrier_semaphore()
    for peers, peer in ((XP, x_peer), (ZP, z_peer), (CP, c_peer)):
        for d in peers:
            pl.semaphore_signal(barrier, inc=1, device_id=peer(d), device_id_type=MESH)

    def send(stage, c, src, dst, to):
        pltpu.make_async_remote_copy(
            src_ref=src, dst_ref=dst, send_sem=send_sem.at[stage, c],
            recv_sem=recv_sem.at[stage, c], device_id=to, device_id_type=MESH,
        ).start()

    def moved(stage, c, view):
        return pltpu.make_async_remote_copy(
            src_ref=view, dst_ref=view, send_sem=send_sem.at[stage, c],
            recv_sem=recv_sem.at[stage, c], device_id=x_peer(1), device_id_type=MESH,
        )

    views = {}
    for c in range(NC):
        views[0, c] = xbuf[c]
        views[1, c] = zbuf[c]
        views[2, c] = ybuf[c].at[pl.ds(1, 7)]
        views[3, c] = rbuf[c]
        views[4, c] = agx[c].at[0, pl.ds(0, 7)]
        views[5, c] = agx[c].at[pl.ds(0, 3)]

    def arrived(stage, c):
        moved(stage, c, views[stage, c]).wait_recv()

    loads[0].wait()
    loads[1].wait()
    logits = jnp.dot(tok[...], sw[...], preferred_element_type=F32)
    group = lax.broadcasted_iota(jnp.int32, (1, SLOTS_ALL), 1) // 4
    masked = []
    for b in range(4):
        named = group == pat_ref[b, 0]
        for j in range(1, 16):
            named = jnp.logical_or(named, group == pat_ref[b, j])
        masked.append(jnp.where(named, logits[b * 128:(b + 1) * 128], LOW))
    turned = jnp.concatenate(masked, axis=0).T
    turned = jnp.concatenate(
        [turned[(zz * XN + xx) * 8:(zz * XN + xx) * 8 + 8] for xx in range(XN) for zz in range(ZN)],
        axis=0,
    )
    top = jnp.maximum(jnp.max(turned, axis=1, keepdims=True), EMPTY)
    weights = jnp.exp(turned - top)
    mass = jnp.sum(weights, axis=1, keepdims=True)
    wt_ref[...] = weights.astype(BF16)
    psend[0][:, CHUNKS[0]:] = ext_of(top, mass).astype(BF16)
    for c in range(NC):
        s, w = STARTS[c], CHUNKS[c]
        part = jnp.dot(wt_ref[...], tok[:, s:s + w], preferred_element_type=F32)
        psend[c][:, 0:w] = part.astype(BF16)
        if c == 0:
            pl.semaphore_wait(barrier, len(XP) + len(ZP) + len(CP))
        for d in XP:
            rows = pl.ds(pl.multiple_of(((x + d) % XN) * 64, 64), 64)
            send(0, c, psend[c].at[rows], xbuf[c].at[d - 1], x_peer(d))

    e = jnp.exp(logits - jnp.max(logits, axis=1, keepdims=True))
    probs[...] = (e / jnp.sum(e, axis=1, keepdims=True)).astype(BF16)

    state = {}

    def stage_x(c):
        w = CHUNKS[c]
        h = w // 2
        arrived(0, c)
        mine = pl.ds(pl.multiple_of(x * 64, 64), 64)
        if c == 0:
            exts = [psend[0][mine, w:]] + [xbuf[0][k, :, w:] for k in range(3)]
            state["x"] = merge([of_ext(e) for e in exts])
        factors, top, mass = state["x"]
        total = factors[0] * psend[c][mine, 0:w].astype(F32)
        for k in range(3):
            total = total + factors[k + 1] * xbuf[c][k, :, 0:w].astype(F32)
        zsend[c][:, :, 0:h] = pack(total.reshape(ZN, 8, w)).astype(BF16)
        if c == 0:
            e = ext_of(top, mass).reshape(ZN, 8, EXT)
            zsend[c][:, :, h:] = jnp.concatenate([e, e], axis=1).astype(BF16)
        for d in ZP:
            send(1, c, zsend[c].at[(z + d) % ZN], zbuf[c].at[d - 1], z_peer(d))

    def stage_z(c):
        h = CHUNKS[c] // 2
        arrived(1, c)
        if c == 0:
            exts = [zsend[0][z, :, h:]] + [zbuf[0][k, :, h:] for k in range(7)]
            factors, _, mass = merge([of_ext(e) for e in exts])
            state["z"] = [f / mass for f in factors]
        factors = state["z"]
        total = factors[0] * zsend[c][z, :, 0:h].astype(F32)
        for k in range(7):
            total = total + factors[k + 1] * zbuf[c][k, :, 0:h].astype(F32)
        ybuf[c][0] = total.astype(BF16)
        for j in CP:
            send(2, c, ybuf[c].at[0], ybuf[c].at[j], c_peer(j))

    def stage_in(c):
        s, w = STARTS[c], CHUNKS[c]
        arrived(2, c)
        if c == 0:
            loads[2].wait()
        rows = unpack(ybuf[c][...]).astype(BF16)
        inner = [jnp.dot(rows, win[e, s:s + w, :], preferred_element_type=F32) for e in range(2)]
        if c == 0:
            state["inner"] = inner
        else:
            state["inner"] = [a + b for a, b in zip(state["inner"], inner)]

    def stage_out(c):
        s, w = STARTS[c], CHUNKS[c]
        if c == 0:
            loads[3].wait()
            first = lax.broadcasted_iota(jnp.int32, (64, FS), 0) % 8 < 4
            act = jax.nn.gelu(jnp.where(first, *state["inner"]), approximate=True)
            state["active"] = [
                jnp.where(first, act, 0.0).astype(BF16), jnp.where(first, 0.0, act).astype(BF16)]
        outer = jnp.dot(state["active"][0], wout[0, :, s:s + w], preferred_element_type=F32)
        outer = outer + jnp.dot(state["active"][1], wout[1, :, s:s + w], preferred_element_type=F32)
        rsend[c][...] = pack(outer.reshape(CLIPS, 8, w)).astype(BF16)
        for j in CP:
            send(3, c, rsend[c].at[j], rbuf[c].at[j - 1], c_back(j))

    def stage_sum(c):
        arrived(3, c)
        total = rsend[c][0].astype(F32)
        for k in range(7):
            total = total + rbuf[c][k].astype(F32)
        agx[c][x, z] = total.astype(BF16)
        for d in ZP:
            send(4, c, agx[c].at[x, z], agx[c].at[x, z], z_peer(d))

    def stage_spread(c):
        arrived(4, c)
        for d in XP:
            send(5, c, agx[c].at[x], agx[c].at[x], x_peer(d))

    def stage_mix(c):
        s, w = STARTS[c], CHUNKS[c]
        arrived(5, c)
        rows = [agx[c][xx].astype(F32) for xx in range(XN)]
        table = jnp.concatenate(
            [jnp.concatenate([rows[xx][zz, :8], rows[xx][zz, 8:]], axis=1)
             for zz in range(ZN) for xx in range(XN)],
            axis=0,
        ).astype(BF16)
        mixed = jnp.dot(probs[...], table, preferred_element_type=F32)
        outv[:, s:s + w] = mixed.astype(BF16)
        pltpu.make_async_copy(
            outv.at[:, pl.ds(s, w)], out_hbm.at[:, pl.ds(s, w)], out_sem.at[c]).start()

    def pipeline(stages):
        n = len(stages)
        for step in range(NC + n - 1):
            for i in range(n):
                if 0 <= step - i < NC:
                    stages[i](step - i)

    pipeline([stage_x, stage_z, stage_in])
    pipeline([stage_out, stage_sum, stage_spread, stage_mix])

    for stage in range(6):
        for c in range(NC):
            moved(stage, c, views[stage, c]).wait_send()
    for c in range(NC):
        s, w = STARTS[c], CHUNKS[c]
        pltpu.make_async_copy(
            outv.at[:, pl.ds(s, w)], out_hbm.at[:, pl.ds(s, w)], out_sem.at[c]).wait()


def local(tokens, slot_weight, pattern, w_in, w_out):
    def vm(*shape):
        return pltpu.VMEM(shape, BF16)

    halves = [w // 2 for w in CHUNKS]
    ext = [EXT if c == 0 else 0 for c in range(NC)]
    scratch = [vm(TOK, D), vm(D, SLOTS_ALL), vm(2, D, FS), vm(2, FS, D)]
    scratch += [vm(SLOTS_ALL, TOK), vm(TOK, SLOTS_ALL), vm(TOK, D)]
    scratch += [vm(SLOTS_ALL, CHUNKS[c] + ext[c]) for c in range(NC)]
    scratch += [vm(3, 64, CHUNKS[c] + ext[c]) for c in range(NC)]
    scratch += [vm(ZN, 16, halves[c] + ext[c]) for c in range(NC)]
    scratch += [vm(7, 16, halves[c] + ext[c]) for c in range(NC)]
    scratch += [vm(CLIPS, 16, halves[c]) for c in range(NC)]
    scratch += [vm(CLIPS, 16, halves[c]) for c in range(NC)]
    scratch += [vm(7, 16, halves[c]) for c in range(NC)]
    scratch += [vm(XN, ZN, 16, halves[c]) for c in range(NC)]
    scratch += [
        pltpu.SemaphoreType.DMA((4,)), pltpu.SemaphoreType.DMA((NC,)),
        pltpu.SemaphoreType.DMA((6, NC)), pltpu.SemaphoreType.DMA((6, NC)),
    ]
    hbm = pl.BlockSpec(memory_space=pl.ANY)
    out = pl.pallas_call(
        kernel,
        out_shape=jax.ShapeDtypeStruct((TOK, D), BF16),
        in_specs=[hbm, hbm, pl.BlockSpec(memory_space=pltpu.SMEM), hbm, hbm],
        out_specs=hbm,
        scratch_shapes=scratch,
        compiler_params=pltpu.CompilerParams(
            collective_id=0, has_side_effects=True, vmem_limit_bytes=56 << 20),
        name="layer",
    )(tokens.reshape(TOK, D), slot_weight, pattern, w_in, w_out)
    return out.reshape(tokens.shape)


def solution(mesh):
    in_specs = (
        P("clip", "seq", None),
        P(),
        P("seq", None),
        P("seq", None, "clip"),
        P("seq", "clip", None),
    )
    return jax.shard_map(
        local, mesh=mesh, in_specs=in_specs, out_specs=P("clip", "seq", None), check_vma=False)
```

time: 669 us -> 53.2 us (0.08)
  the two profiles are of different devices: /device:TPU:2 before, /device:TPU:8 now
where the time goes in v1:
time: 53.2 us; the launch traced here: 53.1 us
  Pallas kernels  50.6 us (95%)
  local copies, waits for them, and re-layouts  2.46 us (5%)
    pallas_call x1, Pallas kernels, local(): pl.pallas_call(kernel, out_shape=jax.ShapeDtypeStruct((TOK, D), BF16), in...  50.6 us
    unnamed x1, local copies, waits for them, and re-layouts  2.46 us

profile of v1, /device:TPU:8, one launch (start us, length us, event | category | flops | bytes accessed | tf_op | source)
XLA Modules:
  0.0 53.1 jit_solution(9037765316426426013)
XLA Ops:
  0.0 50.6 %layer.1 = bf16[512,1280]{1,0:T(8,128)(2,1)} custom-call(bf16[512,1280]{1,0:T(8,128)(2,1)} %bitcast.3, bf16[1280,256]{1,0:T(8,128)(2,1)} %sw_hbm.1, s32[4,16]{1,0:T(4,128)} %pat_ref.1, bf16[2,1280,640]{2,1,0:T(8,128)(2,1)} %win_hbm.1, bf16[2,640,1280]{2,1,0:T(8,128)(2,1)} %wout_hbm.1), custom_call_target="tpu_custom_call" | custom-call | tf_op jit(solution)/shard_map/layer/pallas_call | solution.py:303
  50.7 2.5 %copy.7 = bf16[1,512,1280]{2,1,0:T(8,128)(2,1)} copy(bf16[1,512,1280]{2,1,0:T(8,128)(2,1)} %bitcast.2) | data formatting | bytes 2621440

commit v2 on v1

v2 whole, which is shorter than its diff:
```python
import jax
import jax.numpy as jnp
from jax import lax
from jax.experimental import pallas as pl
from jax.experimental.pallas import tpu as pltpu
from jax.sharding import PartitionSpec as P

MESH = pl.DeviceIdType.MESH
BF16, F32 = jnp.bfloat16, jnp.float32
D = 1280
FS = 640
TOK = 512
SLOTS_ALL = 256
ZN, XN, YN = 8, 4, 4
EXT = 128
CHUNKS = (512, 512, 256)
STARTS = tuple(sum(CHUNKS[:i]) for i in range(len(CHUNKS)))
NC = len(CHUNKS)
ORDER_IN = ((0, 0), (0, 1), (0, 2), (1, 0), (1, 1), (1, 2))
ORDER_OUT = ((0, 0), (0, 1), (0, 2), (1, 0), (1, 1), (1, 2))
PART = 256
LOW = -1.0e30
EMPTY = -1.0e29

XP = (2, 1, 3)
ZP = (4, 3, 5, 2, 6, 1, 7)
YP = (2, 1, 3)


def pieces(v):
    hi = v.astype(BF16).astype(F32)
    mid = (v - hi).astype(BF16).astype(F32)
    lo = ((v - hi) - mid).astype(BF16).astype(F32)
    return hi, mid, lo


def ext_of(top, mass):
    lane = lax.broadcasted_iota(jnp.int32, (top.shape[0], EXT), 1)
    out = jnp.zeros((top.shape[0], EXT), F32)
    for i, piece in enumerate(pieces(top) + pieces(mass)):
        out = jnp.where(lane == i, piece, out)
    return out


def of_ext(ext):
    e = ext.astype(F32)
    return e[:, 0:1] + e[:, 1:2] + e[:, 2:3], e[:, 3:4] + e[:, 4:5] + e[:, 5:6]


def merge(stats):
    top = stats[0][0]
    for t, _ in stats[1:]:
        top = jnp.maximum(top, t)
    factors = [jnp.exp(t - top) for t, _ in stats]
    mass = factors[0] * stats[0][1]
    for f, (_, m) in zip(factors[1:], stats[1:]):
        mass = mass + f * m
    return factors, top, mass


def pack(v):
    h = v.shape[-1] // 2
    return jnp.concatenate([v[:, :, :h], v[:, :, h:]], axis=1)


def kernel(tok_hbm, sw_hbm, pat_hbm, win_hbm, wout_hbm, probs, table_ref, *scratch):
    it = iter(scratch)
    tok, sw, pat, win, wout, wt_ref = (next(it) for _ in range(6))
    psend, xbuf, zsend, zbuf, ybuf, rsend, rbuf, agx = (
        [next(it) for _ in range(NC)] for _ in range(8))
    load_sem, send_sem, recv_sem = next(it), next(it), next(it)

    seq, clip = lax.axis_index("seq"), lax.axis_index("clip")
    z, x = seq // XN, seq % XN
    y, core = clip // 2, clip % 2

    def dev(dz, dx, dy, k):
        return {
            "seq": ((z + dz) % ZN) * XN + (x + dx) % XN, "clip": ((y + dy) % YN) * 2 + k}

    pat_load = pltpu.make_async_copy(pat_hbm, pat, load_sem.at[0])
    sw_load = pltpu.make_async_copy(sw_hbm, sw, load_sem.at[1])
    tok_loads = [
        pltpu.make_async_copy(
            tok_hbm.at[pl.ds(i * PART, PART)], tok.at[pl.ds(i * PART, PART)], load_sem.at[2 + i])
        for i in range(TOK // PART)
    ]
    win_load = pltpu.make_async_copy(win_hbm, win, load_sem.at[6])
    wout_load = pltpu.make_async_copy(wout_hbm, wout, load_sem.at[7])
    sw_load.start()
    for load in tok_loads:
        load.start()
    pat_load.start()

    barrier = pltpu.get_barrier_semaphore()

    def greet(*to):
        pl.semaphore_signal(barrier, inc=1, device_id=dev(*to), device_id_type=MESH)

    for d in XP:
        greet(0, d, 0, 1)
    for d in YP:
        greet(0, 0, d, 1)

    @pl.when(core == 0)
    def _():
        greet(0, 0, 0, 1)

    @pl.when(core == 1)
    def _():
        greet(0, 0, 0, 0)
        for d in XP:
            greet(0, d, 0, 0)
        for d in YP:
            greet(0, 0, d, 0)
        for d in ZP:
            greet(d, 0, 0, 1)

    def send(stage, c, src, dst, to, sent=None):
        pltpu.make_async_remote_copy(
            src_ref=src, dst_ref=dst, send_sem=send_sem.at[stage if sent is None else sent, c],
            recv_sem=recv_sem.at[stage, c], device_id=dev(*to), device_id_type=MESH,
        ).start()

    def moved(stage, c, view):
        return pltpu.make_async_remote_copy(
            src_ref=view, dst_ref=view, send_sem=send_sem.at[stage, c],
            recv_sem=recv_sem.at[min(stage, 5), c], device_id=dev(0, 1, 0, 1), device_id_type=MESH,
        )

    sw_load.wait()
    logits = []
    for i in range(TOK // PART):
        tok_loads[i].wait()
        logits.append(
            jnp.dot(tok[i * PART:(i + 1) * PART], sw[...], preferred_element_type=F32))
    logits = jnp.concatenate(logits, axis=0)
    win_load.start()
    wout_load.start()
    pat_load.wait()
    group = lax.broadcasted_iota(jnp.int32, (1, SLOTS_ALL), 1) // 4
    masked = []
    for b in range(4):
        named = group == pat[b, 0]
        for j in range(1, 16):
            named = jnp.logical_or(named, group == pat[b, j])
        masked.append(jnp.where(named, logits[b * 128:(b + 1) * 128], LOW))
    turned = jnp.concatenate(masked, axis=0).T
    turned = jnp.concatenate(
        [turned[(zz * XN + xx) * 8:(zz * XN + xx) * 8 + 8] for xx in range(XN) for zz in range(ZN)],
        axis=0,
    )
    top = jnp.maximum(jnp.max(turned, axis=1, keepdims=True), EMPTY)
    weights = jnp.exp(turned - top)
    mass = jnp.sum(weights, axis=1, keepdims=True)
    wt_ref[...] = weights.astype(BF16)
    psend[0][:, CHUNKS[0]:] = ext_of(top, mass).astype(BF16)
    for c in range(NC):
        s, w = STARTS[c], CHUNKS[c]
        part = jnp.dot(wt_ref[...], tok[:, s:s + w], preferred_element_type=F32)
        psend[c][:, 0:w] = part.astype(BF16)

        @pl.when(core == 0)
        def _():
            if c == 0:
                pl.semaphore_wait(barrier, 7)
            for d in XP + (0,):
                rows = pl.ds(pl.multiple_of(((x + d) % XN) * 64, 64), 64)
                send(0, c, psend[c].at[rows], xbuf[c].at[3 + d], (0, d, 0, 1))

        @pl.when(core == 1)
        def _():
            if c == 0:
                pl.semaphore_wait(barrier, 20)
            for d in XP:
                rows = pl.ds(pl.multiple_of(((x + d) % XN) * 64, 64), 64)
                send(0, c, psend[c].at[rows], xbuf[c].at[d - 1], (0, d, 0, 1))

    e = jnp.exp(logits - jnp.max(logits, axis=1, keepdims=True))
    probs[...] = (e / jnp.sum(e, axis=1, keepdims=True)).astype(BF16)

    state = {}

    def stage_x(c):
        w = CHUNKS[c]
        mine = pl.ds(pl.multiple_of(x * 64, 64), 64)
        moved(0, c, xbuf[c]).wait_recv()

        def sources(lanes):
            return (
                [xbuf[c][k, :, lanes] for k in range(3, 7)],
                [psend[c][mine, lanes]] + [xbuf[c][k, :, lanes] for k in range(3)],
            )

        if c == 0:
            state["x"] = [merge([of_ext(e) for e in exts]) for exts in sources(slice(w, w + EXT))]
            exts = [ext_of(t, m).reshape(ZN, 8, EXT) for _, t, m in state["x"]]
            zsend[0][:, :, w:] = jnp.concatenate(exts, axis=1).astype(BF16)
        totals = []
        for (factors, _, _), parts in zip(state["x"], sources(slice(0, w))):
            total = factors[0] * parts[0].astype(F32)
            for f, p in zip(factors[1:], parts[1:]):
                total = total + f * p.astype(F32)
            totals.append(total.reshape(ZN, 8, w))
        zsend[c][:, :, 0:w] = jnp.concatenate(totals, axis=1).astype(BF16)
        for d in ZP:
            send(1, c, zsend[c].at[(z + d) % ZN], zbuf[c].at[d - 1], (d, 0, 0, 1))

    def stage_z(c):
        w = CHUNKS[c]
        moved(1, c, zbuf[c]).wait_recv()
        if c == 0:
            exts = [zsend[0][z, :, w:]] + [zbuf[0][k, :, w:] for k in range(7)]
            factors, _, mass = merge([of_ext(e) for e in exts])
            state["z"] = [f / mass for f in factors]
        factors = state["z"]
        total = factors[0] * zsend[c][z, :, 0:w].astype(F32)
        for k in range(7):
            total = total + factors[k + 1] * zbuf[c][k, :, 0:w].astype(F32)
        ybuf[c][0] = total.astype(BF16)
        for d in YP:
            send(2, c, ybuf[c].at[0], ybuf[c].at[d], (0, 0, d, 0))
        send(2, c, ybuf[c].at[0], ybuf[c].at[0], (0, 0, 0, 0))
        for d in YP:
            send(2, c, ybuf[c].at[0], ybuf[c].at[d], (0, 0, d, 1))

    def stage_in(c):
        s, w = STARTS[c], CHUNKS[c]

        @pl.when(core == 0)
        def _():
            moved(2, c, ybuf[c]).wait_recv()

        @pl.when(core == 1)
        def _():
            moved(2, c, ybuf[c].at[pl.ds(1, 3)]).wait_recv()

        if c == 0:
            win_load.wait()
        rows = ybuf[c][...].reshape(64, w)
        inner = [jnp.dot(rows, win[e, s:s + w, :], preferred_element_type=F32) for e in range(2)]
        if c == 0:
            state["inner"] = inner
        else:
            state["inner"] = [a + b for a, b in zip(state["inner"], inner)]

    def stage_out(c):
        s, w = STARTS[c], CHUNKS[c]
        if c == 0:
            wout_load.wait()
            first = lax.broadcasted_iota(jnp.int32, (64, FS), 0) % 8 < 4
            act = jax.nn.gelu(jnp.where(first, *state["inner"]), approximate=True)
            state["active"] = [
                jnp.where(first, act, 0.0).astype(BF16), jnp.where(first, 0.0, act).astype(BF16)]
        outer = jnp.dot(state["active"][0], wout[0, :, s:s + w], preferred_element_type=F32)
        outer = outer + jnp.dot(state["active"][1], wout[1, :, s:s + w], preferred_element_type=F32)
        rsend[c][...] = outer.reshape(YN, 16, w).astype(BF16)

        @pl.when(core == 0)
        def _():
            for d in YP + (0,):
                send(3, c, rsend[c].at[d], rbuf[c].at[3 + d], (0, 0, YN - d, 1))

        @pl.when(core == 1)
        def _():
            for d in YP:
                send(3, c, rsend[c].at[d], rbuf[c].at[d - 1], (0, 0, YN - d, 1))

    def stage_sum(c):
        w = CHUNKS[c]
        moved(3, c, rbuf[c]).wait_recv()
        total = rsend[c][0].astype(F32)
        for k in range(7):
            total = total + rbuf[c][k].astype(F32)
        agx[c][x, z] = pack(total.reshape(2, 8, w)).astype(BF16)
        for d in ZP:
            send(4, c, agx[c].at[x, z], agx[c].at[x, z], (d, 0, 0, 1))

    def stage_spread(c):
        moved(4, c, agx[c].at[0, pl.ds(0, 7)]).wait_recv()
        for d in XP:
            send(5, c, agx[c].at[x, :, 0], agx[c].at[x, :, 0], (0, d, 0, 0), 6)
            send(5, c, agx[c].at[x, :, 1], agx[c].at[x, :, 1], (0, d, 0, 1))
        send(5, c, agx[c].at[x, :, 0], agx[c].at[x, :, 0], (0, 0, 0, 0), 6)

    def stage_mix(c):
        s, w = STARTS[c], CHUNKS[c]

        @pl.when(core == 0)
        def _():
            moved(5, c, agx[c].at[:, :, 0]).wait_recv()

        @pl.when(core == 1)
        def _():
            moved(5, c, agx[c].at[pl.ds(0, 3), :, 0]).wait_recv()

        rows = [agx[c][xx, :, core].astype(F32) for xx in range(XN)]
        table_ref[:, s:s + w] = jnp.concatenate(
            [jnp.concatenate([rows[xx][zz, :8], rows[xx][zz, 8:]], axis=1)
             for zz in range(ZN) for xx in range(XN)],
            axis=0,
        ).astype(BF16)

    @pl.when(core == 1)
    def _():
        for stage, c in ORDER_IN:
            (stage_x, stage_z)[stage](c)

    for c in range(NC):
        stage_in(c)
    for c in range(NC):
        stage_out(c)

    @pl.when(core == 1)
    def _():
        for stage, c in ORDER_OUT:
            (stage_sum, stage_spread)[stage](c)

    for c in range(NC):
        stage_mix(c)

    @pl.when(core == 0)
    def _():
        for c in range(NC):
            moved(0, c, xbuf[c].at[pl.ds(0, 4)]).wait_send()
            moved(3, c, rbuf[c].at[pl.ds(0, 4)]).wait_send()

    @pl.when(core == 1)
    def _():
        for c in range(NC):
            moved(0, c, xbuf[c].at[pl.ds(0, 3)]).wait_send()
            moved(1, c, zbuf[c]).wait_send()
            moved(2, c, rbuf[c]).wait_send()
            moved(3, c, rbuf[c].at[pl.ds(0, 3)]).wait_send()
            moved(4, c, agx[c].at[0, pl.ds(0, 7)]).wait_send()
            moved(5, c, agx[c].at[pl.ds(0, 3), :, 0]).wait_send()
            moved(6, c, agx[c].at[:, :, 0]).wait_send()


def local(tokens, slot_weight, pattern, w_in, w_out):
    def vm(*shape):
        return pltpu.VMEM(shape, BF16)

    ext = [EXT if c == 0 else 0 for c in range(NC)]
    scratch = [
        vm(TOK, D), vm(D, SLOTS_ALL), pltpu.SMEM((4, 16), jnp.int32),
        vm(2, D, FS), vm(2, FS, D), vm(SLOTS_ALL, TOK)]
    scratch += [vm(SLOTS_ALL, w + e) for w, e in zip(CHUNKS, ext)]
    scratch += [vm(7, 64, w + e) for w, e in zip(CHUNKS, ext)]
    scratch += [vm(ZN, 16, w + e) for w, e in zip(CHUNKS, ext)]
    scratch += [vm(7, 16, w + e) for w, e in zip(CHUNKS, ext)]
    scratch += [vm(YN, 16, w) for w in CHUNKS]
    scratch += [vm(YN, 16, w) for w in CHUNKS]
    scratch += [vm(7, 16, w) for w in CHUNKS]
    scratch += [vm(XN, ZN, 2, 16, w // 2) for w in CHUNKS]
    scratch += [
        pltpu.SemaphoreType.DMA((8,)),
        pltpu.SemaphoreType.DMA((7, NC)), pltpu.SemaphoreType.DMA((6, NC)),
    ]
    hbm = pl.BlockSpec(memory_space=pltpu.HBM)
    vmem = pl.BlockSpec(memory_space=pltpu.VMEM)
    probs, table = pl.pallas_call(
        kernel,
        out_shape=(
            jax.ShapeDtypeStruct((TOK, SLOTS_ALL), BF16),
            jax.ShapeDtypeStruct((SLOTS_ALL, D), BF16),
        ),
        in_specs=[hbm, hbm, hbm, hbm, hbm],
        out_specs=(vmem, vmem),
        scratch_shapes=scratch,
        compiler_params=pltpu.CompilerParams(
            collective_id=0, has_side_effects=True, vmem_limit_bytes=53 << 20),
        name="layer",
    )(tokens.reshape(TOK, D), slot_weight, pattern, w_in, w_out)
    mixed = jnp.dot(probs, table, preferred_element_type=F32).astype(BF16)
    return mixed.reshape(tokens.shape)


def solution(mesh):
    in_specs = (
        P("clip", "seq", None),
        P(),
        P("seq", None),
        P("seq", None, "clip"),
        P("seq", "clip", None),
    )
    return jax.shard_map(
        local, mesh=mesh, in_specs=in_specs, out_specs=P("clip", "seq", None), check_vma=False)
```

time: 53.2 us -> 46.3 us (0.87)
  the two profiles are of different devices: /device:TPU:8 before, /device:TPU:1 now
where the time goes in v2:
time: 46.3 us; the launch traced here: 46.2 us
  Pallas kernels  44 us (95%)
  matrix products  1.57 us (3%)
  local copies, waits for them, and re-layouts  0.68 us (1%)
    pallas_call x1, Pallas kernels, local(): pl.pallas_call(kernel, out_shape=(jax.ShapeDtypeStruct((TOK, SLOTS_ALL),...  44 us
    dot_general x1, matrix products, local(): mixed = jnp.dot(probs, table, preferred_element_type=F32).astype(BF16)  1.57 us

profile of v2, /device:TPU:1, one launch (start us, length us, event | category | flops | bytes accessed | tf_op | source)
XLA Modules:
  0.0 46.2 jit_solution(9486926863719622422)
XLA Ops:
  0.0 0.0 copy-start
  0.0 0.7 %copy-done = s32[4,16]{1,0:T(4,128)S(1)} copy-done((s32[4,16]{1,0:T(4,128)S(1)}, s32[4,16]{1,0:T(4,128)}, u32[]{:S(2)}) %copy-start) | copy-done | bytes 280
  0.7 44.0 %layer.1 = (bf16[512,256]{1,0:T(8,128)(2,1)S(1)}, bf16[256,1280]{1,0:T(8,128)(2,1)S(1)}) custom-call(bf16[512,1280]{1,0:T(8,128)(2,1)} %bitcast.5, bf16[1280,256]{1,0:T(8,128)(2,1)} %sw_hbm.1, s32[4,16]{1,0:T(4,128)S(1)} %copy-done, bf16[2,1280,640]{2,1,0:T(8,128)(2,1)} %win_hbm.1, bf16[2,640,1280]{2,1,0:T(8,128)(2,1)} %wout_hbm.1), custom_call_target="tpu_custom_call" | custom-call | tf_op jit(solution)/shard_map/layer/pallas_call | solution.py:362
  44.7 1.6 %fusion = bf16[1,512,1280]{2,1,0:T(8,128)(2,1)} fusion(bf16[512,256]{1,0:T(8,128)(2,1)S(1)} %get-tuple-element.7, bf16[256,1280]{1,0:T(8,128)(2,1)S(1)} %get-tuple-element.8), kind=kOutput, calls=%fused_computation.1 | convolution fusion | flops 336199680 | bytes 2228224 | tf_op jit(solution)/shard_map/dot_general | solution.py:375
Async XLA Ops:
  0.0 0.7 %copy-start = (s32[4,16]{1,0:T(4,128)S(1)}, s32[4,16]{1,0:T(4,128)}, u32[]{:S(2)}) copy-start(s32[4,16]{1,0:T(4,128)} %pat_hbm.1) | copy-start | bytes 772

commit v3 on v2

v3 whole, which is shorter than its diff:
```python
import jax
import jax.numpy as jnp
from jax import lax
from jax.experimental import pallas as pl
from jax.experimental.pallas import tpu as pltpu
from jax.sharding import PartitionSpec as P

MESH = pl.DeviceIdType.MESH
BF16, F32 = jnp.bfloat16, jnp.float32
D = 1280
FS = 640
TOK = 512
SLOTS_ALL = 256
ZN, XN, YN = 8, 4, 4
EXT = 128
IN = (256, 512, 256, 256)
IN_AT = tuple(sum(IN[:i]) for i in range(len(IN)))
OUT = (256, 256, 512, 256)
OUT_AT = tuple(sum(OUT[:i]) for i in range(len(OUT)))
NC = 3
ORDER = (0, 1, NC, 2)
RING = (0, 1, 7, 2, 6, 3, 5, 4)
FAR_FIRST = (7, 5, 6, 4, 3, 1, 2)
HALF = 4
NEAR = 5
(X_NEAR, X_FAR, Z_IN, SHARE, REDUCE, Z_NEAR, Z_FAR, S_NEAR, S_FAR, S_OWN) = range(10)
PARTS = {S_OWN: (0, 1), S_NEAR: (1, NEAR - 1), S_FAR: (NEAR, ZN - NEAR)}
LOW = -1.0e30
EMPTY = -1.0e29

XP = (2, 1, 3)
ZP = (4, 3, 5, 2, 6, 1, 7)
YP = (2, 1, 3)


def groups():
    recv, sent = {}, {}
    for c in range(NC + 1):
        for stage in range(S_OWN):
            if c < NC or stage not in (X_FAR, Z_FAR, S_FAR):
                recv[stage, c] = len(recv)
        recv[S_OWN, c] = recv[S_NEAR, c]
        for stage in range(S_OWN + 1):
            if stage in (SHARE, REDUCE):
                sent[stage, c] = 2
            elif c == NC:
                sent[stage, c] = 3 if stage == S_NEAR else 1
            else:
                sent[stage, c] = 0 if stage < SHARE else 3
    return recv, sent


RECV, SENT = groups()
RECV_COUNT = max(RECV.values()) + 1
WA, WB = sum(IN[:NC]) + EXT, IN[NC] + EXT
OA, OB = sum(OUT[:NC]), OUT[NC]
SENT_ALL = (
    ((256, WA), (256, WB), (64, D)),
    ((3 * 64 + 7 * 16, WA), (7 * 32 + 3 * 16 + 48 * OB // WB, WB), (160, D),
     ((7 * 80 * OA + 15 * 32 * OB) // D, D)),
)


def pieces(v):
    hi = v.astype(BF16).astype(F32)
    mid = (v - hi).astype(BF16).astype(F32)
    lo = ((v - hi) - mid).astype(BF16).astype(F32)
    return hi, mid, lo


def ext_of(top, mass):
    lane = lax.broadcasted_iota(jnp.int32, (top.shape[0], EXT), 1)
    out = jnp.zeros((top.shape[0], EXT), F32)
    for i, piece in enumerate(pieces(top) + pieces(mass)):
        out = jnp.where(lane == i, piece, out)
    return out


def of_ext(ext):
    e = ext.astype(F32)
    return e[:, 0:1] + e[:, 1:2] + e[:, 2:3], e[:, 3:4] + e[:, 4:5] + e[:, 5:6]


def merge(stats):
    top = stats[0][0]
    for t, _ in stats[1:]:
        top = jnp.maximum(top, t)
    factors = [jnp.exp(t - top) for t, _ in stats]
    mass = factors[0] * stats[0][1]
    for f, (_, m) in zip(factors[1:], stats[1:]):
        mass = mass + f * m
    return factors, top, mass


def pack(v):
    h = v.shape[-1] // 2
    return jnp.concatenate([v[:, :, :h], v[:, :, h:]], axis=1)


def regroup(v):
    return jnp.concatenate(
        [v[(xx * ZN + p) * 8:(xx * ZN + p) * 8 + 8] for p in range(ZN) for xx in range(XN)],
        axis=0,
    )


def weigh(factors, parts):
    total = factors[0] * parts[0].astype(F32)
    for f, p in zip(factors[1:], parts[1:]):
        total = total + f * p.astype(F32)
    return total


def kernel(tok_hbm, sw_hbm, pat_hbm, win_hbm, wout_hbm, mixed, *scratch):
    it = iter(scratch)
    tok, sw, pat, win, wout, turned, wt_ref, probs, table_ref = (next(it) for _ in range(9))
    psend, xbuf, zsend, zbuf = ([next(it) for _ in range(NC)] for _ in range(4))
    ybuf, rsend, rbuf = ([next(it) for _ in range(NC + 1)] for _ in range(3))
    agx = [next(it) for _ in range(NC)]
    qsend, qbuf, rsx, rbx, agz = (next(it) for _ in range(5))
    load_sem, send_sem, recv_sem = next(it), next(it), next(it)

    seq, clip = lax.axis_index("seq"), lax.axis_index("clip")
    z, x = seq // XN, seq % XN
    y, core = clip // 2, clip % 2

    def dev(dz, dx, dy, k):
        return {
            "seq": ((z + dz) % ZN) * XN + (x + dx) % XN, "clip": ((y + dy) % YN) * 2 + k}

    loads = [
        pltpu.make_async_copy(src, dst, load_sem.at[i])
        for i, (src, dst) in enumerate((
            (sw_hbm, sw), (tok_hbm, tok), (pat_hbm, pat), (win_hbm, win), (wout_hbm, wout)))
    ]
    for load in loads[:3]:
        load.start()

    barrier = pltpu.get_barrier_semaphore()

    def greet(*to):
        pl.semaphore_signal(barrier, inc=1, device_id=dev(*to), device_id_type=MESH)

    for d in XP:
        greet(0, d, 0, 1)
    for d in YP:
        greet(0, 0, d, 1)
    for d in RING[1:]:
        greet(d, 0, 0, 1)

    @pl.when(core == 0)
    def _():
        greet(0, 0, 0, 1)

    @pl.when(core == 1)
    def _():
        greet(0, 0, 0, 0)
        for d in XP:
            greet(0, d, 0, 0)
        for d in YP:
            greet(0, 0, d, 0)
        for d in RING[1:]:
            greet(d, 0, 0, 0)

    def send(stage, c, src, dst, to):
        pltpu.make_async_remote_copy(
            src_ref=src, dst_ref=dst, send_sem=send_sem.at[SENT[stage, c]],
            recv_sem=recv_sem.at[RECV[stage, c]], device_id=dev(*to), device_id_type=MESH,
        ).start()

    def moved(stage, c, view):
        return pltpu.make_async_remote_copy(
            src_ref=view, dst_ref=view, send_sem=send_sem.at[SENT[stage, c]],
            recv_sem=recv_sem.at[RECV[stage, c]], device_id=dev(0, 1, 0, 1),
            device_id_type=MESH,
        )

    def drain(k):
        for i, (rows, lanes) in enumerate(SENT_ALL[k]):
            view = wout.at[pl.ds(0, rows), pl.ds(0, lanes)]
            pltpu.make_async_remote_copy(
                src_ref=view, dst_ref=view, send_sem=send_sem.at[i], recv_sem=recv_sem.at[0],
                device_id=dev(0, 1, 0, 1), device_id_type=MESH,
            ).wait_send()

    loads[0].wait()
    loads[1].wait()
    logits = jnp.dot(tok[...], sw[...], preferred_element_type=F32)
    loads[3].start()
    loads[4].start()
    loads[2].wait()
    group = lax.broadcasted_iota(jnp.int32, (1, SLOTS_ALL), 1) // 4
    masked = []
    for b in range(4):
        named = group == pat[b, 0]
        for j in range(1, 16):
            named = jnp.logical_or(named, group == pat[b, j])
        masked.append(jnp.where(named, logits[b * 128:(b + 1) * 128], LOW))
    turned[...] = jnp.concatenate(masked, axis=0).T
    places = [(z + d) % ZN for d in RING]
    rows = jnp.concatenate(
        [turned[pl.ds(pl.multiple_of(zz * 32 + xx * 8, 8), 8), :]
         for xx in range(XN) for zz in places],
        axis=0,
    )
    top = jnp.maximum(jnp.max(rows, axis=1, keepdims=True), EMPTY)
    weights = jnp.exp(rows - top)
    mass = jnp.sum(weights, axis=1, keepdims=True)
    wt_ref[...] = weights.astype(BF16)
    ext = ext_of(top, mass)
    psend[0][:, IN[0]:] = ext.astype(BF16)
    qsend[:, IN[NC]:] = regroup(ext).astype(BF16)

    def send_x(stage, c):
        at = 32 if stage == X_FAR else 0
        part = pl.ds(at, 32)

        def rows(d):
            return psend[c].at[pl.ds(pl.multiple_of(((x + d) % XN) * 64 + at, 32), 32)]

        @pl.when(core == 0)
        def _():
            for d in XP + (0,):
                send(stage, c, rows(d), xbuf[c].at[3 + d, part], (0, d, 0, 1))

        @pl.when(core == 1)
        def _():
            for d in XP:
                send(stage, c, rows(d), xbuf[c].at[d - 1, part], (0, d, 0, 1))

    for c in range(NC):
        s, w = IN_AT[c], IN[c]
        part = jnp.dot(wt_ref[...], tok[:, s:s + w], preferred_element_type=F32)
        psend[c][:, 0:w] = part.astype(BF16)
        if c == 0:
            @pl.when(core == 0)
            def _():
                pl.semaphore_wait(barrier, 14)

            @pl.when(core == 1)
            def _():
                pl.semaphore_wait(barrier, 27)

        send_x(X_FAR, c)
        if c == 0:
            send_x(X_NEAR, c)
            part = jnp.dot(wt_ref[...], tok[:, IN_AT[NC]:], preferred_element_type=F32)
            qsend[:, 0:IN[NC]] = regroup(part).astype(BF16)

            @pl.when(core == 0)
            def _():
                for p in FAR_FIRST + (0,):
                    send(X_NEAR, NC, qsend.at[pl.ds(32 * p, 32)], qbuf.at[7 + p],
                         (RING[p], 0, 0, 1))

            @pl.when(core == 1)
            def _():
                for p in FAR_FIRST:
                    send(X_NEAR, NC, qsend.at[pl.ds(32 * p, 32)], qbuf.at[p - 1],
                         (RING[p], 0, 0, 1))

    for c in range(1, NC):
        send_x(X_NEAR, c)

    e = jnp.exp(logits - jnp.max(logits, axis=1, keepdims=True))
    probs[...] = (e / jnp.sum(e, axis=1, keepdims=True)).astype(BF16)

    state = {}

    def stage_x(stage, c):
        w = IN[c]
        at = 32 if stage == X_FAR else 0
        half = pl.ds(at // 8, HALF)
        part = slice(at, at + 32)
        mine = pl.ds(pl.multiple_of(x * 64 + at, 32), 32)
        moved(stage, c, xbuf[c].at[:, pl.ds(at, 32)]).wait_recv()

        def sources(lanes):
            return (
                [xbuf[c][k, part, lanes] for k in range(3, 7)],
                [psend[c][mine, lanes]] + [xbuf[c][k, part, lanes] for k in range(3)],
            )

        if c == 0:
            state[stage] = [merge([of_ext(e) for e in exts]) for exts in sources(slice(w, w + EXT))]
            exts = [ext_of(t, m).reshape(HALF, 8, EXT) for _, t, m in state[stage]]
            zsend[0][half, :, w:] = jnp.concatenate(exts, axis=1).astype(BF16)
        totals = [
            weigh(factors, parts).reshape(HALF, 8, w)
            for (factors, _, _), parts in zip(state[stage], sources(slice(0, w)))
        ]
        zsend[c][half, :, 0:w] = jnp.concatenate(totals, axis=1).astype(BF16)
        for p in FAR_FIRST:
            if (p >= HALF) == (stage == X_FAR):
                send(Z_IN, c, zsend[c].at[p], zbuf[c].at[p - 1], (RING[p], 0, 0, 1))

    def stage_z(c):
        w = IN[c]
        moved(Z_IN, c, zbuf[c]).wait_recv()
        if c == 0:
            exts = [zsend[0][0, :, w:]] + [zbuf[0][k, :, w:] for k in range(7)]
            factors, _, mass = merge([of_ext(e) for e in exts])
            state["z"] = [f / mass for f in factors]
        parts = [zsend[c][0, :, 0:w]] + [zbuf[c][k, :, 0:w] for k in range(7)]
        share(c, weigh(state["z"], parts))

    def stage_qz():
        w = IN[NC]
        moved(X_NEAR, NC, qbuf).wait_recv()
        merged, totals = [], []
        for parts in (
            [qbuf[k] for k in range(7, 15)],
            [qsend[0:32, :]] + [qbuf[k] for k in range(7)],
        ):
            factors, top, mass = merge([of_ext(p[:, w:]) for p in parts])
            merged.append(ext_of(top, mass).reshape(XN, 8, EXT))
            totals.append(weigh(factors, [p[:, 0:w] for p in parts]).reshape(XN, 8, w))
        rsx[:, :, 0:w] = jnp.concatenate(totals, axis=1).astype(BF16)
        rsx[:, :, w:] = jnp.concatenate(merged, axis=1).astype(BF16)
        for d in XP:
            send(Z_IN, NC, rsx.at[(x + d) % XN], rbx.at[d - 1], (0, d, 0, 1))

    def stage_qx():
        w = IN[NC]
        moved(Z_IN, NC, rbx).wait_recv()
        parts = [rsx[x]] + [rbx[k] for k in range(3)]
        factors, _, mass = merge([of_ext(p[:, w:]) for p in parts])
        share(NC, weigh([f / mass for f in factors], [p[:, 0:w] for p in parts]))

    def share(c, total):
        ybuf[c][0] = total.astype(BF16)
        for d in YP:
            send(SHARE, c, ybuf[c].at[0], ybuf[c].at[d], (0, 0, d, 0))
        send(SHARE, c, ybuf[c].at[0], ybuf[c].at[0], (0, 0, 0, 0))
        for d in YP:
            send(SHARE, c, ybuf[c].at[0], ybuf[c].at[d], (0, 0, d, 1))

    def stage_in(c):
        s, w = IN_AT[c], IN[c]

        @pl.when(core == 0)
        def _():
            moved(SHARE, c, ybuf[c]).wait_recv()

        @pl.when(core == 1)
        def _():
            moved(SHARE, c, ybuf[c].at[pl.ds(1, 3)]).wait_recv()

        if c == 0:
            loads[3].wait()
        rows = ybuf[c][...].reshape(64, w)
        inner = [jnp.dot(rows, win[e, s:s + w, :], preferred_element_type=F32) for e in range(2)]
        if c == 0:
            state["inner"] = inner
        else:
            state["inner"] = [a + b for a, b in zip(state["inner"], inner)]

    def stage_out(c):
        s, w = OUT_AT[c], OUT[c]
        if c == 0:
            loads[4].wait()
            first = lax.broadcasted_iota(jnp.int32, (64, FS), 0) % 8 < 4
            act = jax.nn.gelu(jnp.where(first, *state["inner"]), approximate=True)
            state["active"] = jnp.concatenate(
                [jnp.where(first, act, 0.0), jnp.where(first, 0.0, act)], axis=1).astype(BF16)
        if c < 2:
            lanes = slice(0, OUT[0]) if c == 0 else slice(OUT[0], D)
            state["outer"] = jnp.dot(
                state["active"], wout[:, lanes], preferred_element_type=F32)
            state["at"] = lanes.start
        outer = state["outer"][:, s - state["at"]:s - state["at"] + w]
        rsend[c][...] = outer.reshape(YN, 16, w).astype(BF16)

        @pl.when(core == 0)
        def _():
            for d in YP + (0,):
                send(REDUCE, c, rsend[c].at[d], rbuf[c].at[3 + d], (0, 0, YN - d, 1))

        @pl.when(core == 1)
        def _():
            for d in YP:
                send(REDUCE, c, rsend[c].at[d], rbuf[c].at[d - 1], (0, 0, YN - d, 1))

    def stage_sum(c):
        w = OUT[c]
        moved(REDUCE, c, rbuf[c]).wait_recv()
        total = rsend[c][0].astype(F32)
        for k in range(7):
            total = total + rbuf[c][k].astype(F32)
        total = pack(total.reshape(2, 8, w)).astype(BF16)
        if c == NC:
            agz[z, x] = total
            for d in XP:
                send(Z_NEAR, NC, agz.at[z, x], agz.at[z, x], (0, d, 0, 1))
        else:
            agx[c][x, 0] = total
            for p in range(1, NEAR):
                send(Z_NEAR, c, agx[c].at[x, 0], agx[c].at[x, p], (ZN - RING[p], 0, 0, 1))
            spread(S_OWN, c)
            for p in range(NEAR, ZN):
                send(Z_FAR, c, agx[c].at[x, 0], agx[c].at[x, p], (ZN - RING[p], 0, 0, 1))

    def stage_spread_z():
        moved(Z_NEAR, NC, agz.at[0, pl.ds(0, 3)]).wait_recv()
        for p in FAR_FIRST:
            send(S_NEAR, NC, agz.at[z, :, 0], agz.at[z, :, 0], (RING[p], 0, 0, 0))
            send(S_NEAR, NC, agz.at[z, :, 1], agz.at[z, :, 1], (RING[p], 0, 0, 1))
        send(S_NEAR, NC, agz.at[z, :, 0], agz.at[z, :, 0], (0, 0, 0, 0))

    def stage_near(c):
        moved(Z_NEAR, c, agx[c].at[0, pl.ds(1, NEAR - 1)]).wait_recv()
        spread(S_NEAR, c)

    def stage_far(c):
        moved(Z_FAR, c, agx[c].at[0, pl.ds(NEAR, ZN - NEAR)]).wait_recv()
        spread(S_FAR, c)

    def spread(stage, c):
        places = pl.ds(*PARTS[stage])
        for d in XP:
            part = agx[c].at[x, places, 0]
            send(stage, c, part, part, (0, d, 0, 0))
            part = agx[c].at[x, places, 1]
            send(stage, c, part, part, (0, d, 0, 1))
        part = agx[c].at[x, places, 0]
        send(stage, c, part, part, (0, 0, 0, 0))

    def stage_mix_z():
        @pl.when(core == 0)
        def _():
            moved(S_NEAR, NC, agz.at[:, :, 0]).wait_recv()

        @pl.when(core == 1)
        def _():
            moved(S_NEAR, NC, agz.at[pl.ds(0, 7), :, 0]).wait_recv()

        rows = agz[:, :, core].astype(F32).reshape(ZN * XN, 16, OUT[NC] // 2)
        table_ref[:, OUT_AT[NC]:] = jnp.concatenate(
            [rows[:, :8], rows[:, 8:]], axis=2).reshape(SLOTS_ALL, OUT[NC]).astype(BF16)

    def stage_mix(stage, c):
        s, w = OUT_AT[c], OUT[c]
        first, count = PARTS[stage]
        if stage == S_NEAR:
            first, count = 0, NEAR

        @pl.when(core == 0)
        def _():
            moved(stage, c, agx[c].at[:, pl.ds(first, count), 0]).wait_recv()

        @pl.when(core == 1)
        def _():
            moved(stage, c, agx[c].at[pl.ds(0, 3), pl.ds(first, count), 0]).wait_recv()

        for p in range(first, first + count):
            rows = agx[c][:, p, core].astype(F32)
            at = pl.ds(pl.multiple_of(places[p] * 32, 32), 32)
            table_ref[at, s:s + w] = jnp.concatenate(
                [rows[:, :8], rows[:, 8:]], axis=2).reshape(32, w).astype(BF16)

    @pl.when(core == 1)
    def _():
        stage_x(X_FAR, 0)
        stage_x(X_NEAR, 0)
        stage_x(X_FAR, 1)
        stage_x(X_FAR, 2)
        stage_x(X_NEAR, 1)
        stage_z(0)
        stage_x(X_NEAR, 2)
        stage_qz()
        stage_z(1)
        stage_qx()
        stage_z(2)

    for c in ORDER:
        stage_in(c)
    for c in ORDER:
        stage_out(c)

    @pl.when(core == 1)
    def _():
        for c in ORDER:
            stage_sum(c)
        stage_near(0)
        stage_near(1)
        stage_spread_z()
        stage_far(0)
        stage_near(2)
        stage_far(1)
        stage_far(2)

    stage_mix(S_NEAR, 0)
    stage_mix(S_NEAR, 1)

    def finish(c):
        lanes = slice(OUT_AT[c], OUT_AT[c] + OUT[c])
        mixed[:, lanes] = jnp.dot(
            probs[...], table_ref[:, lanes], preferred_element_type=F32).astype(BF16)

    stage_mix(S_FAR, 0)
    finish(0)
    stage_mix_z()
    finish(NC)
    stage_mix(S_NEAR, 2)
    stage_mix(S_FAR, 1)
    finish(1)
    stage_mix(S_FAR, 2)
    finish(2)

    @pl.when(core == 0)
    def _():
        drain(0)

    @pl.when(core == 1)
    def _():
        drain(1)


def local(tokens, slot_weight, pattern, w_in, w_out):
    def vm(*shape):
        return pltpu.VMEM(shape, BF16)

    first = [w + (EXT if c == 0 else 0) for c, w in enumerate(IN[:NC])]
    scratch = [
        vm(TOK, D), vm(D, SLOTS_ALL), pltpu.SMEM((4, 16), jnp.int32),
        vm(2, D, FS), vm(2 * FS, D), pltpu.VMEM((SLOTS_ALL, TOK), F32), vm(SLOTS_ALL, TOK),
        vm(TOK, SLOTS_ALL), vm(SLOTS_ALL, D)]
    scratch += [vm(SLOTS_ALL, w) for w in first]
    scratch += [vm(7, 64, w) for w in first]
    scratch += [vm(ZN, 16, w) for w in first]
    scratch += [vm(7, 16, w) for w in first]
    scratch += [vm(YN, 16, w) for w in IN]
    scratch += [vm(YN, 16, w) for w in OUT]
    scratch += [vm(7, 16, w) for w in OUT]
    scratch += [vm(XN, ZN, 2, 16, w // 2) for w in OUT[:NC]]
    last = IN[NC] + EXT
    scratch += [
        vm(SLOTS_ALL, last), vm(15, 32, last), vm(XN, 16, last), vm(3, 16, last),
        vm(ZN, XN, 2, 16, OUT[NC] // 2),
        pltpu.SemaphoreType.DMA((5,)),
        pltpu.SemaphoreType.DMA((4,)), pltpu.SemaphoreType.DMA((RECV_COUNT,)),
    ]
    arrays = (tokens.reshape(TOK, D), slot_weight, pattern, w_in, w_out.reshape(2 * FS, D))
    hbm = pl.BlockSpec(memory_space=pltpu.HBM)
    vmem = pl.BlockSpec(memory_space=pltpu.VMEM)
    mixed = pl.pallas_call(
        kernel,
        out_shape=pltpu.VMEM((TOK, D), BF16),
        in_specs=[hbm, hbm, hbm, hbm, hbm],
        out_specs=vmem,
        scratch_shapes=scratch,
        compiler_params=pltpu.CompilerParams(
            collective_id=0, has_side_effects=True, vmem_limit_bytes=40 << 20),
        name="layer",
    )(*(pltpu.with_memory_space_constraint(a, pltpu.HBM) for a in arrays))
    return mixed.reshape(tokens.shape)


def solution(mesh):
    in_specs = (
        P("clip", "seq", None),
        P(),
        P("seq", None),
        P("seq", None, "clip"),
        P("seq", "clip", None),
    )
    return jax.shard_map(
        local, mesh=mesh, in_specs=in_specs, out_specs=P("clip", "seq", None), check_vma=False)
```

time: 46.3 us -> 41.4 us (0.89)
  Pallas kernels: 44 us -> 40.2 us
  matrix products: 1.57 us -> 0 us
    pallas_call x1, Pallas kernels: 44 us -> 40.2 us  [local(): pl.pallas_call(kernel, out_shape=pltpu.VMEM((TOK, D), BF16), in_specs=[hb...]
    dot_general x1 -> x0, matrix products: 1.57 us -> none  [local(): mixed = jnp.dot(probs, table, preferred_element_type=F32).astype(BF16)]
    unnamed x2 -> x1, local copies, waits for them, and re-layouts: 0.68 us -> 1.06 us
where the time goes in v3:
time: 41.4 us; the launch traced here: 41.3 us
  Pallas kernels  40.2 us (97%)
  local copies, waits for them, and re-layouts  1.06 us (3%)
    pallas_call x1, Pallas kernels, local(): pl.pallas_call(kernel, out_shape=pltpu.VMEM((TOK, D), BF16), in_specs=[hb...  40.2 us
    unnamed x1, local copies, waits for them, and re-layouts  1.06 us

profile of v3, /device:TPU:1, one launch (start us, length us, event | category | flops | bytes accessed | tf_op | source)
XLA Modules:
  0.0 41.3 jit_solution(9781555444075048172)
XLA Ops:
  0.0 40.2 %layer.1 = bf16[512,1280]{1,0:T(8,128)(2,1)S(1)} custom-call(bf16[512,1280]{1,0:T(8,128)(2,1)} %bitcast.5, bf16[1280,256]{1,0:T(8,128)(2,1)} %sw_hbm.1, s32[4,16]{1,0:T(4,128)} %pat_hbm.1, bf16[2,1280,640]{2,1,0:T(8,128)(2,1)} %win_hbm.1, bf16[1280,1280]{1,0:T(8,128)(2,1)} %bitcast.4), custom_call_target="tpu_custom_call" | custom-call | tf_op jit(solution)/shard_map/layer/pallas_call | solution.py:546
  40.2 1.1 %copy.7 = bf16[1,512,1280]{2,1,0:T(8,128)(2,1)} copy(bf16[1,512,1280]{2,1,0:T(8,128)(2,1)S(1)} %bitcast.3) | data formatting | bytes 2621440

commit v4 on v3

--- a/solution.py
+++ b/solution.py
@@ -23,7 +23,7 @@
 FAR_FIRST = (7, 5, 6, 4, 3, 1, 2)
 HALF = 4
 NEAR = 5
-(X_NEAR, X_FAR, Z_IN, SHARE, REDUCE, Z_NEAR, Z_FAR, S_NEAR, S_FAR, S_OWN) = range(10)
+(X_NEAR, X_FAR, Z_IN, SHARE, REDUCE, Z_NEAR, Z_FAR, S_NEAR, S_FAR, S_OWN, STATS) = range(11)
 PARTS = {S_OWN: (0, 1), S_NEAR: (1, NEAR - 1), S_FAR: (NEAR, ZN - NEAR)}
 LOW = -1.0e30
 EMPTY = -1.0e29
@@ -38,26 +38,30 @@
     for c in range(NC + 1):
         for stage in range(S_OWN):
             if c < NC or stage not in (X_FAR, Z_FAR, S_FAR):
-                recv[stage, c] = len(recv)
+                recv[stage, c] = len(set(recv.values()))
         recv[S_OWN, c] = recv[S_NEAR, c]
-        for stage in range(S_OWN + 1):
+        if c in (0, NC):
+            recv[STATS, c] = len(set(recv.values()))
+        for stage in range(STATS + 1):
             if stage in (SHARE, REDUCE):
                 sent[stage, c] = 2
             elif c == NC:
                 sent[stage, c] = 3 if stage == S_NEAR else 1
             else:
-                sent[stage, c] = 0 if stage < SHARE else 3
+                sent[stage, c] = 0 if stage < SHARE or stage == STATS else 3
     return recv, sent
 
 
 RECV, SENT = groups()
 RECV_COUNT = max(RECV.values()) + 1
-WA, WB = sum(IN[:NC]) + EXT, IN[NC] + EXT
-OA, OB = sum(OUT[:NC]), OUT[NC]
+WA, OA = sum(IN[:NC]), sum(OUT[:NC])
+WB, OB = IN[NC], OUT[NC]
 SENT_ALL = (
-    ((256, WA), (256, WB), (64, D)),
-    ((3 * 64 + 7 * 16, WA), (7 * 32 + 3 * 16 + 48 * OB // WB, WB), (160, D),
-     ((7 * 80 * OA + 15 * 32 * OB) // D, D)),
+    (4 * 4 * WA // 128 + 4, 8 * 2 * WB // 128 + 8, 4 * D // 128),
+    (3 * 4 * WA // 128 + 3 + 7 * (WA + EXT) // 128,
+     7 * 2 * WB // 128 + 7 + 3 * (WB + EXT) // 128 + 3 * OB // 128,
+     10 * D // 128,
+     (7 * 5 * OA + 15 * 2 * OB) // 128),
 )
 
 
@@ -79,6 +83,15 @@
 def of_ext(ext):
     e = ext.astype(F32)
     return e[:, 0:1] + e[:, 1:2] + e[:, 2:3], e[:, 3:4] + e[:, 4:5] + e[:, 5:6]
+
+
+def as_tiles(ext):
+    t = ext.T[:16]
+    return jnp.stack([t[:, :128], t[:, 128:]]).astype(BF16)
+
+
+def of_tiles(tiles):
+    return tiles.reshape(-1, 128).astype(F32).T
 
 
 def merge(stats):
@@ -117,7 +130,7 @@
     psend, xbuf, zsend, zbuf = ([next(it) for _ in range(NC)] for _ in range(4))
     ybuf, rsend, rbuf = ([next(it) for _ in range(NC + 1)] for _ in range(3))
     agx = [next(it) for _ in range(NC)]
-    qsend, qbuf, rsx, rbx, agz = (next(it) for _ in range(5))
+    qsend, qbuf, rsx, rbx, agz, xstat, xstats, qstat, qstats, yard = (next(it) for _ in range(10))
     load_sem, send_sem, recv_sem = next(it), next(it), next(it)
 
     seq, clip = lax.axis_index("seq"), lax.axis_index("clip")
@@ -176,8 +189,8 @@
         )
 
     def drain(k):
-        for i, (rows, lanes) in enumerate(SENT_ALL[k]):
-            view = wout.at[pl.ds(0, rows), pl.ds(0, lanes)]
+        for i, tiles in enumerate(SENT_ALL[k]):
+            view = yard.at[pl.ds(0, tiles)]
             pltpu.make_async_remote_copy(
                 src_ref=view, dst_ref=view, send_sem=send_sem.at[i], recv_sem=recv_sem.at[0],
                 device_id=dev(0, 1, 0, 1), device_id_type=MESH,
@@ -208,8 +221,6 @@
     mass = jnp.sum(weights, axis=1, keepdims=True)
     wt_ref[...] = weights.astype(BF16)
     ext = ext_of(top, mass)
-    psend[0][:, IN[0]:] = ext.astype(BF16)
-    qsend[:, IN[NC]:] = regroup(ext).astype(BF16)
 
     def send_x(stage, c):
         at = 32 if stage == X_FAR else 0
@@ -244,8 +255,25 @@
         send_x(X_FAR, c)
         if c == 0:
             send_x(X_NEAR, c)
+            xstat[...] = as_tiles(ext)
+            qstat[...] = as_tiles(regroup(ext))
+
+            @pl.when(core == 0)
+            def _():
+                for d in XP + (0,):
+                    send(STATS, 0, xstat.at[(x + d) % XN // 2], xstats.at[3 + d], (0, d, 0, 1))
+                for p in FAR_FIRST + (0,):
+                    send(STATS, NC, qstat.at[p // 4], qstats.at[7 + p], (RING[p], 0, 0, 1))
+
+            @pl.when(core == 1)
+            def _():
+                for d in XP:
+                    send(STATS, 0, xstat.at[(x + d) % XN // 2], xstats.at[d - 1], (0, d, 0, 1))
+                for p in FAR_FIRST:
+                    send(STATS, NC, qstat.at[p // 4], qstats.at[p - 1], (RING[p], 0, 0, 1))
+
             part = jnp.dot(wt_ref[...], tok[:, IN_AT[NC]:], preferred_element_type=F32)
-            qsend[:, 0:IN[NC]] = regroup(part).astype(BF16)
+            qsend[...] = regroup(part).astype(BF16)
 
             @pl.when(core == 0)
             def _():
@@ -275,19 +303,23 @@
         mine = pl.ds(pl.multiple_of(x * 64 + at, 32), 32)
         moved(stage, c, xbuf[c].at[:, pl.ds(at, 32)]).wait_recv()
 
-        def sources(lanes):
-            return (
-                [xbuf[c][k, part, lanes] for k in range(3, 7)],
-                [psend[c][mine, lanes]] + [xbuf[c][k, part, lanes] for k in range(3)],
-            )
-
+        sources = (
+            [xbuf[c][k, part] for k in range(3, 7)],
+            [psend[c][mine]] + [xbuf[c][k, part] for k in range(3)],
+        )
+        if c == 0 and stage == X_FAR:
+            moved(STATS, 0, xstats).wait_recv()
+            t = of_tiles(jnp.concatenate([xstats[...], xstat[x // 2][None]]))
+            t = jnp.where(x % 2 == 0, t[:64], t[64:])
+            state["stats"] = [t[:, 16 * k:16 * k + 16] for k in (3, 4, 5, 6, 7, 0, 1, 2)]
         if c == 0:
-            state[stage] = [merge([of_ext(e) for e in exts]) for exts in sources(slice(w, w + EXT))]
+            stats = [of_ext(t[part]) for t in state["stats"]]
+            state[stage] = [merge(stats[:4]), merge(stats[4:])]
             exts = [ext_of(t, m).reshape(HALF, 8, EXT) for _, t, m in state[stage]]
             zsend[0][half, :, w:] = jnp.concatenate(exts, axis=1).astype(BF16)
         totals = [
             weigh(factors, parts).reshape(HALF, 8, w)
-            for (factors, _, _), parts in zip(state[stage], sources(slice(0, w)))
+            for (factors, _, _), parts in zip(state[stage], sources)
         ]
         zsend[c][half, :, 0:w] = jnp.concatenate(totals, axis=1).astype(BF16)
         for p in FAR_FIRST:
@@ -304,19 +336,29 @@
         parts = [zsend[c][0, :, 0:w]] + [zbuf[c][k, :, 0:w] for k in range(7)]
         share(c, weigh(state["z"], parts))
 
+    def stage_qstats():
+        moved(STATS, NC, qstats).wait_recv()
+        t = of_tiles(jnp.concatenate([qstats[...], qstat[0:1]]))
+        stats = [
+            of_ext(t[32 * (p % 4):32 * (p % 4) + 32, 16 * k:16 * k + 16])
+            for p, k in [(p, 7 + p) for p in range(8)] + [(0, 15)] + [(p, p - 1) for p in range(1, 8)]
+        ]
+        state["q"] = [merge(stats[:8]), merge(stats[8:])]
+        merged = [ext_of(top, mass).reshape(XN, 8, EXT) for _, top, mass in state["q"]]
+        rsx[:, :, IN[NC]:] = jnp.concatenate(merged, axis=1).astype(BF16)
+
     def stage_qz():
         w = IN[NC]
         moved(X_NEAR, NC, qbuf).wait_recv()
-        merged, totals = [], []
-        for parts in (
+        sources = (
             [qbuf[k] for k in range(7, 15)],
             [qsend[0:32, :]] + [qbuf[k] for k in range(7)],
-        ):
-            factors, top, mass = merge([of_ext(p[:, w:]) for p in parts])
-            merged.append(ext_of(top, mass).reshape(XN, 8, EXT))
-            totals.append(weigh(factors, [p[:, 0:w] for p in parts]).reshape(XN, 8, w))
+        )
+        totals = [
+            weigh(factors, parts).reshape(XN, 8, w)
+            for (factors, _, _), parts in zip(state["q"], sources)
+        ]
         rsx[:, :, 0:w] = jnp.concatenate(totals, axis=1).astype(BF16)
-        rsx[:, :, w:] = jnp.concatenate(merged, axis=1).astype(BF16)
         for d in XP:
             send(Z_IN, NC, rsx.at[(x + d) % XN], rbx.at[d - 1], (0, d, 0, 1))
 
@@ -464,10 +506,11 @@
         stage_x(X_NEAR, 0)
         stage_x(X_FAR, 1)
         stage_x(X_FAR, 2)
+        stage_qstats()
         stage_x(X_NEAR, 1)
-        stage_z(0)
         stage_x(X_NEAR, 2)
         stage_qz()
+        stage_z(0)
         stage_z(1)
         stage_qx()
         stage_z(2)
@@ -525,8 +568,8 @@
         vm(TOK, D), vm(D, SLOTS_ALL), pltpu.SMEM((4, 16), jnp.int32),
         vm(2, D, FS), vm(2 * FS, D), pltpu.VMEM((SLOTS_ALL, TOK), F32), vm(SLOTS_ALL, TOK),
         vm(TOK, SLOTS_ALL), vm(SLOTS_ALL, D)]
-    scratch += [vm(SLOTS_ALL, w) for w in first]
-    scratch += [vm(7, 64, w) for w in first]
+    scratch += [vm(SLOTS_ALL, w) for w in IN[:NC]]
+    scratch += [vm(7, 64, w) for w in IN[:NC]]
     scratch += [vm(ZN, 16, w) for w in first]
     scratch += [vm(7, 16, w) for w in first]
     scratch += [vm(YN, 16, w) for w in IN]
@@ -535,8 +578,10 @@
     scratch += [vm(XN, ZN, 2, 16, w // 2) for w in OUT[:NC]]
     last = IN[NC] + EXT
     scratch += [
-        vm(SLOTS_ALL, last), vm(15, 32, last), vm(XN, 16, last), vm(3, 16, last),
+        vm(SLOTS_ALL, IN[NC]), vm(15, 32, IN[NC]), vm(XN, 16, last), vm(3, 16, last),
         vm(ZN, XN, 2, 16, OUT[NC] // 2),
+        vm(2, 16, 128), vm(7, 16, 128), vm(2, 16, 128), vm(15, 16, 128),
+        vm(max(max(tiles) for tiles in SENT_ALL), 16, 128),
         pltpu.SemaphoreType.DMA((5,)),
         pltpu.SemaphoreType.DMA((4,)), pltpu.SemaphoreType.DMA((RECV_COUNT,)),
     ]

time: 41.4 us -> 40.6 us (0.981)
  Pallas kernels: 40.2 us -> 39.4 us
    pallas_call x1, Pallas kernels: 40.2 us -> 39.4 us  [local(): pl.pallas_call(kernel, out_shape=pltpu.VMEM((TOK, D), BF16), in_specs=[hb...]
where the time goes in v4:
time: 40.6 us; the launch traced here: 40.5 us
  Pallas kernels  39.4 us (97%)
  local copies, waits for them, and re-layouts  1.06 us (3%)
    pallas_call x1, Pallas kernels, local(): pl.pallas_call(kernel, out_shape=pltpu.VMEM((TOK, D), BF16), in_specs=[hb...  39.4 us
    unnamed x1, local copies, waits for them, and re-layouts  1.06 us

profile of v4, /device:TPU:1, one launch (start us, length us, event | category | flops | bytes accessed | tf_op | source)
XLA Modules:
  0.0 40.5 jit_solution(7096753424709987139)
XLA Ops:
  0.0 39.4 %layer.1 = bf16[512,1280]{1,0:T(8,128)(2,1)S(1)} custom-call(bf16[512,1280]{1,0:T(8,128)(2,1)} %bitcast.5, bf16[1280,256]{1,0:T(8,128)(2,1)} %sw_hbm.1, s32[4,16]{1,0:T(4,128)} %pat_hbm.1, bf16[2,1280,640]{2,1,0:T(8,128)(2,1)} %win_hbm.1, bf16[1280,1280]{1,0:T(8,128)(2,1)} %bitcast.4), custom_call_target="tpu_custom_call" | custom-call | tf_op jit(solution)/shard_map/layer/pallas_call | solution.py:591
  39.4 1.1 %copy.7 = bf16[1,512,1280]{2,1,0:T(8,128)(2,1)} copy(bf16[1,512,1280]{2,1,0:T(8,128)(2,1)S(1)} %bitcast.3) | data formatting | bytes 2621440

commit v5 on v4

--- a/solution.py
+++ b/solution.py
@@ -196,20 +196,28 @@
                 device_id=dev(0, 1, 0, 1), device_id_type=MESH,
             ).wait_send()
 
+    loads[2].wait()
+    group = lax.broadcasted_iota(jnp.int32, (1, SLOTS_ALL), 1) // 4
+    named = []
+    for b in range(4):
+        found = group == pat[b, 0]
+        for j in range(1, 16):
+            found = jnp.logical_or(found, group == pat[b, j])
+        named.append(jnp.where(found, 1.0, 0.0))
     loads[0].wait()
     loads[1].wait()
-    logits = jnp.dot(tok[...], sw[...], preferred_element_type=F32)
     loads[3].start()
     loads[4].start()
-    loads[2].wait()
-    group = lax.broadcasted_iota(jnp.int32, (1, SLOTS_ALL), 1) // 4
-    masked = []
-    for b in range(4):
-        named = group == pat[b, 0]
-        for j in range(1, 16):
-            named = jnp.logical_or(named, group == pat[b, j])
-        masked.append(jnp.where(named, logits[b * 128:(b + 1) * 128], LOW))
-    turned[...] = jnp.concatenate(masked, axis=0).T
+    logits = []
+    for i in range(2):
+        rows = slice(i * 256, i * 256 + 256)
+        logits.append(jnp.dot(tok[rows], sw[...], preferred_element_type=F32))
+        masked = [
+            jnp.where(named[2 * i + b] > 0.5, logits[i][b * 128:(b + 1) * 128], LOW)
+            for b in range(2)
+        ]
+        turned[:, rows] = jnp.concatenate(masked, axis=0).T
+    logits = jnp.concatenate(logits, axis=0)
     places = [(z + d) % ZN for d in RING]
     rows = jnp.concatenate(
         [turned[pl.ds(pl.multiple_of(zz * 32 + xx * 8, 8), 8), :]

time: 40.6 us -> 40.5 us (level)
  no operation moved by 1% of the time
where the time goes in v5:
time: 40.5 us; the launch traced here: 40.4 us
  Pallas kernels  39.3 us (97%)
  local copies, waits for them, and re-layouts  1.06 us (3%)
    pallas_call x1, Pallas kernels, local(): pl.pallas_call(kernel, out_shape=pltpu.VMEM((TOK, D), BF16), in_specs=[hb...  39.3 us
    unnamed x1, local copies, waits for them, and re-layouts  1.06 us

profile of v5, /device:TPU:1, one launch (start us, length us, event | category | flops | bytes accessed | tf_op | source)
XLA Modules:
  0.0 40.4 jit_solution(2457678219953879611)
XLA Ops:
  0.0 39.3 %layer.1 = bf16[512,1280]{1,0:T(8,128)(2,1)S(1)} custom-call(bf16[512,1280]{1,0:T(8,128)(2,1)} %bitcast.5, bf16[1280,256]{1,0:T(8,128)(2,1)} %sw_hbm.1, s32[4,16]{1,0:T(4,128)} %pat_hbm.1, bf16[2,1280,640]{2,1,0:T(8,128)(2,1)} %win_hbm.1, bf16[1280,1280]{1,0:T(8,128)(2,1)} %bitcast.4), custom_call_target="tpu_custom_call" | custom-call | tf_op jit(solution)/shard_map/layer/pallas_call | solution.py:599
  39.3 1.1 %copy.7 = bf16[1,512,1280]{2,1,0:T(8,128)(2,1)} copy(bf16[1,512,1280]{2,1,0:T(8,128)(2,1)S(1)} %bitcast.3) | data formatting | bytes 2621440

commit v6 on v5

--- a/solution.py
+++ b/solution.py
@@ -446,9 +446,9 @@
             agx[c][x, 0] = total
             for p in range(1, NEAR):
                 send(Z_NEAR, c, agx[c].at[x, 0], agx[c].at[x, p], (ZN - RING[p], 0, 0, 1))
+            for p in range(ZN - 1, NEAR - 1, -1):
+                send(Z_FAR, c, agx[c].at[x, 0], agx[c].at[x, p], (ZN - RING[p], 0, 0, 1))
             spread(S_OWN, c)
-            for p in range(NEAR, ZN):
-                send(Z_FAR, c, agx[c].at[x, 0], agx[c].at[x, p], (ZN - RING[p], 0, 0, 1))
 
     def stage_spread_z():
         moved(Z_NEAR, NC, agz.at[0, pl.ds(0, 3)]).wait_recv()

time: 40.5 us -> 40.5 us (level)
  no operation moved by 1% of the time
where the time goes in v6:
time: 40.5 us; the launch traced here: 40.4 us
  Pallas kernels  39.3 us (97%)
  local copies, waits for them, and re-layouts  1.06 us (3%)
    pallas_call x1, Pallas kernels, local(): pl.pallas_call(kernel, out_shape=pltpu.VMEM((TOK, D), BF16), in_specs=[hb...  39.3 us
    unnamed x1, local copies, waits for them, and re-layouts  1.06 us

profile of v6, /device:TPU:1, one launch (start us, length us, event | category | flops | bytes accessed | tf_op | source)
XLA Modules:
  0.0 40.4 jit_solution(8276914101148948538)
XLA Ops:
  0.0 39.3 %layer.1 = bf16[512,1280]{1,0:T(8,128)(2,1)S(1)} custom-call(bf16[512,1280]{1,0:T(8,128)(2,1)} %bitcast.5, bf16[1280,256]{1,0:T(8,128)(2,1)} %sw_hbm.1, s32[4,16]{1,0:T(4,128)} %pat_hbm.1, bf16[2,1280,640]{2,1,0:T(8,128)(2,1)} %win_hbm.1, bf16[1280,1280]{1,0:T(8,128)(2,1)} %bitcast.4), custom_call_target="tpu_custom_call" | custom-call | tf_op jit(solution)/shard_map/layer/pallas_call | solution.py:599
  39.3 1.1 %copy.7 = bf16[1,512,1280]{2,1,0:T(8,128)(2,1)} copy(bf16[1,512,1280]{2,1,0:T(8,128)(2,1)S(1)} %bitcast.3) | data formatting | bytes 2621440
